TPU v7x, 32 devices: a whole 2x2x4 slice. The times are simulated.
32 devices in a mesh: groups: 2 (over y), expert: 16 (over z, x, core), head: 1.
Axes of the slice: x: 2, y: 2, z: 4, core: 2. Of those that a mesh axis runs over, the one named last changes fastest.
Arguments:
- tokens: bfloat16 [512, 2048], P(('groups', 'expert', 'head')), parts along dimension 0, may hold values from -6 to 6
- norm_gain: float32 [2048], replicated, may hold values from 0.1 to 1.9
- expert_ids: int32 [512, 8], P(('groups', 'expert', 'head')), parts along dimension 0, may hold values from 0 to 15, all different within a row; in each aligned block of 16 rows (0 to 15, 16 to 31, ...) at most 8 rows name the same one
- gate_values: float32 [512, 8], P(('groups', 'expert', 'head')), parts along dimension 0, may hold values from 0.1 to 1
- w_gate: bfloat16 [16, 2048, 768], P('expert', None, 'head'), may hold values from -0.125 to 0.125
- w_up: bfloat16 [16, 2048, 768], P('expert', None, 'head'), may hold values from -0.125 to 0.125
- w_down: bfloat16 [16, 2048, 768], P('expert', None, 'head'), may hold values from -0.21875 to 0.21875
Outputs:
- mixed: bfloat16 [512, 2048], P(('groups', 'expert', 'head')), parts along dimension 0
There are 2 independent parts, one for each index of `groups`. A program takes and returns all parts, laid end to end along the dimension named above; an argument that names none is the same for every part. Nothing has to cross between parts.
Inputs may be any that keep to these rules, and one draw needn't show every extreme that they name: `expert_ids`: each row names 8 different experts. Among the 16 rows of one device no expert is named more than 8 times, a bound that some block reaches.
All inputs are finite; a program needn't handle non-finite values.
Results may differ from a plain program's by a relative error of at most 0.007.
Values may be sent and summed in bfloat16 or wider, within the bound.
A program may use at most 64 MiB of HBM per device.

v0:
```python
import jax
import jax.numpy as jnp
from jax import lax
from jax.sharding import PartitionSpec as P


def expert_apply(rows_in, gate_part, up_part, down_part):
    gate = jnp.dot(rows_in, gate_part, preferred_element_type=jnp.float32)
    upper = jnp.dot(rows_in, up_part, preferred_element_type=jnp.float32)
    hidden = (jax.nn.silu(gate) * upper).astype(jnp.bfloat16)
    return lax.dot_general(
        hidden, down_part, (((1,), (1,)), ((), ())), preferred_element_type=jnp.float32
    )


def per_device(tokens, norm_gain, expert_ids, gate_values, w_gate, w_up, w_down):
    rows, width = tokens.shape
    top = expert_ids.shape[1]
    expert_count = lax.axis_size("expert")
    capacity = max(2, top * rows // expert_count)
    tokens_f = tokens.astype(jnp.float32)
    scale = lax.rsqrt(jnp.mean(tokens_f * tokens_f, axis=-1, keepdims=True) + 1e-06)
    normed = (tokens_f * scale * norm_gain[None, :]).astype(jnp.bfloat16)
    flat_ids = expert_ids.reshape(-1)
    routes_here = flat_ids.shape[0]
    picks = (flat_ids[:, None] == jnp.arange(expert_count, dtype=jnp.int32)[None, :]).astype(
        jnp.bfloat16
    )
    order = jnp.arange(routes_here, dtype=jnp.int32)
    lower = (order[:, None] > order[None, :]).astype(jnp.bfloat16)
    earlier = jnp.dot(lower, picks, preferred_element_type=jnp.float32)
    slot = jnp.sum(earlier * picks.astype(jnp.float32), axis=1).astype(jnp.int32)
    position = flat_ids * capacity + slot
    place = (
        position[:, None] == jnp.arange(expert_count * capacity, dtype=jnp.int32)[None, :]
    ).astype(jnp.bfloat16)
    repeated = jnp.repeat(normed, top, axis=0)
    outgoing = lax.dot_general(
        place, repeated, (((0,), (0,)), ((), ())), preferred_element_type=jnp.float32
    )
    outgoing = outgoing.astype(jnp.bfloat16).reshape(expert_count, capacity, width)
    received = lax.all_to_all(outgoing, "expert", split_axis=0, concat_axis=0, tiled=True)
    count = received.shape[1]
    paired = lax.all_gather(received, "head", axis=0, tiled=True)
    partial_value = expert_apply(paired.reshape(-1, width), w_gate[0], w_up[0], w_down[0])
    partial_value = partial_value.reshape(paired.shape[0], count, width)
    result = lax.psum_scatter(partial_value, "head", scatter_dimension=0, tiled=True).astype(
        jnp.bfloat16
    )
    answered = lax.all_to_all(result, "expert", split_axis=0, concat_axis=0, tiled=True)
    per_route = jnp.dot(place, answered.reshape(-1, width), preferred_element_type=jnp.float32)
    weighted = per_route.reshape(rows, top, width) * gate_values[:, :, None]
    return jnp.sum(weighted, axis=1).astype(jnp.bfloat16)


def solution(mesh):
    in_specs = (
        P(("groups", "expert", "head"), None),
        P(),
        P(("groups", "expert", "head"), None),
        P(("groups", "expert", "head"), None),
        P("expert", None, "head"),
        P("expert", None, "head"),
        P("expert", None, "head"),
    )
    out_specs = P(("groups", "expert", "head"), None)
    return jax.shard_map(
        per_device, mesh=mesh, in_specs=in_specs, out_specs=out_specs, check_vma=False
    )
```

profile of v0, /device:TPU:0, one launch (start us, length us, event | category | flops | bytes accessed | tf_op | source)
XLA Modules:
  0.0 53.9 jit_solution(1421533374488154607)
XLA Ops:
  0.0 0.0 copy-start
  0.0 0.9 %copy.11 = s32[16,8]{1,0:T(8,128)S(1)} copy(s32[16,8]{0,1:T(8,128)} %param.9) | data formatting | bytes 1024 | tf_op args[2]
  0.9 0.1 eq.46
  1.0 0.2 fusion.20
  1.2 1.0 %fusion.35 = f32[16]{0:T(128)S(1)} fusion(bf16[16,2048]{1,0:T(8,128)(2,1)} %param.7), kind=kLoop, calls=%fused_computation.29 | loop fusion | flops 98288 | bytes 65600 | tf_op jit(solution)/shard_map/reduce_sum | solution.py:22
  2.2 0.9 %fusion.37 = bf16[16,2048]{1,0:T(8,128)(2,1)S(1)} fusion(bf16[16,2048]{1,0:T(8,128)(2,1)} %param.7, f32[2048]{0:T(1024)} %param.8, f32[16]{0:T(128)S(1)} %add_rsqrt_fusion), kind=kLoop, calls=%fused_computation.31 | loop fusion | flops 131072 | bytes 139328 | tf_op jit(solution)/shard_map/convert_element_type | solution.py:23
  3.1 0.4 fusion.9
  3.5 21.6 %all_to_all.10 = bf16[16,8,2048]{2,1,0:T(8,128)(2,1)S(1)} all-to-all(bf16[16,8,2048]{2,1,0:T(8,128)(2,1)S(1)} %fusion.9), channel_id=1, replica_groups=mesh['groups'=2,'expert'=16,'head'=1] {'expert'}, dimensions={0} | all-to-all | bytes 1048576 | tf_op jit(solution)/shard_map/all_to_all | solution.py:42
  25.1 0.0 copy-start.1
  25.1 0.8 %copy-done.1 = bf16[16,8,2048]{2,1,0:T(8,128)(2,1)} copy-done((bf16[16,8,2048]{2,1,0:T(8,128)(2,1)}, bf16[16,8,2048]{2,1,0:T(8,128)(2,1)S(1)}, u32[]{:S(2)}) %copy-start.1) | copy-done | bytes 524312
  26.0 2.5 %fusion.4 = f32[128,768]{1,0:T(8,128)S(1)} fusion(bf16[1,2048,768]{2,1,0:T(8,128)(2,1)} %param.11, bf16[16,8,2048]{2,1,0:T(8,128)(2,1)S(1)} %all_to_all.10), kind=kOutput, calls=%fused_computation.4 | convolution fusion | flops 402653184 | bytes 4063232 | tf_op jit(solution)/shard_map/dot_general | solution.py:8
  28.4 0.0 copy-done
  28.5 0.0 copy-start.2
  28.5 4.5 %fusion.6 = bf16[16,8,2048]{2,1,0:T(8,128)(2,1)} fusion(bf16[1,2048,768]{2,1,0:T(8,128)(2,1)S(1)} %copy-done, bf16[1,2048,768]{2,1,0:T(8,128)(2,1)} %param.12, bf16[16,8,2048]{2,1,0:T(8,128)(2,1)} %copy-done.1, f32[128,768]{1,0:T(8,128)S(1)} %fusion.4), kind=kOutput, calls=%fused_computation.7 | convolution fusion | flops 806158336 | bytes 7733248 | tf_op jit(solution)/shard_map/dot_general | solution.py:11
  33.0 4.2 %all-to-all-start.1 = ((bf16[16,8,2048]{2,1,0:T(8,128)(2,1)}), bf16[16,8,2048]{2,1,0:T(8,128)(2,1)}, u32[]{:S(2)}, u32[]{:S(2)}) async-start(bf16[16,8,2048]{2,1,0:T(8,128)(2,1)} %fusion.6), calls=%async_computation.1 | async-start | bytes 1048576 | tf_op jit(solution)/shard_map/all_to_all | solution.py:50
  37.2 0.1 convert_element_type.40
  37.3 0.0 copy-done.2
  37.3 0.1 copy.13
  37.4 14.3 %all-to-all-done.1 = bf16[16,8,2048]{2,1,0:T(8,128)(2,1)} async-done(((bf16[16,8,2048]{2,1,0:T(8,128)(2,1)}), bf16[16,8,2048]{2,1,0:T(8,128)(2,1)}, u32[]{:S(2)}, u32[]{:S(2)}) %all-to-all-start.1) | async-done | bytes 524320 | tf_op jit(solution)/shard_map/all_to_all | solution.py:50
  51.7 2.2 %fusion.10 = bf16[16,2048]{1,0:T(8,128)(2,1)} fusion(bf16[16,8,2048]{2,1,0:T(8,128)(2,1)} %all-to-all-done.1, f32[16,8]{1,0:T(8,128)S(1)} %copy.13, s32[16,8]{1,0:T(8,128)S(1)} %multiply_add_fusion), kind=kOutput, calls=%fused_computation.10 | convolution fusion | flops 67616768 | bytes 590848 | tf_op jit(solution)/shard_map/dot_general | solution.py:51
  (4 shorter events, 0.0 us)
Async XLA Ops:
  0.0 28.4 %copy-start = (bf16[1,2048,768]{2,1,0:T(8,128)(2,1)S(1)}, bf16[1,2048,768]{2,1,0:T(8,128)(2,1)}, u32[]{:S(2)}) copy-start(bf16[1,2048,768]{2,1,0:T(8,128)(2,1)} %param.13) | copy-start | bytes 9437188
  25.1 0.8 %copy-start.1 = (bf16[16,8,2048]{2,1,0:T(8,128)(2,1)}, bf16[16,8,2048]{2,1,0:T(8,128)(2,1)S(1)}, u32[]{:S(2)}) copy-start(bf16[16,8,2048]{2,1,0:T(8,128)(2,1)S(1)} %all_to_all.10) | copy-start | bytes 1572868
  28.5 8.9 %copy-start.2 = (f32[16,8]{0,1:T(8,128)S(1)}, f32[16,8]{0,1:T(8,128)}, u32[]{:S(2)}) copy-start(f32[16,8]{0,1:T(8,128)} %param.10) | copy-start | bytes 1540
  33.0 18.7 %all-to-all-start.1 = ((bf16[16,8,2048]{2,1,0:T(8,128)(2,1)}), bf16[16,8,2048]{2,1,0:T(8,128)(2,1)}, u32[]{:S(2)}, u32[]{:S(2)}) async-start(bf16[16,8,2048]{2,1,0:T(8,128)(2,1)} %fusion.6), calls=%async_computation.1 | async-start | bytes 1048576 | tf_op jit(solution)/shard_map/all_to_all | solution.py:50
where the time goes:
time: 54.3 us; the launch traced here: 53.9 us
  blocking collectives  21.6 us (40%)
  waiting for transfers between devices  14.3 us (26%)
  matrix products  9.74 us (18%)
  starting transfers between devices  4.24 us (8%)
  local copies, waits for them, and re-layouts  1.97 us (4%)
  other arithmetic  1.94 us (4%)
    all_to_all x1, blocking collectives, per_device(): lax.all_to_all(outgoing, 'expert', split_axis=0, concat_axis=0, tiled=True)  21.6 us
    all_to_all x1, waiting for transfers between devices, per_device(): lax.all_to_all(result, 'expert', split_axis=0, concat_axis=0, tiled=True)  14.3 us
    dot_general x1, matrix products, expert_apply(): lax.dot_general(hidden, down_part, (((1,), (1,)), ((), ())), preferred_el...  4.51 us
    all_to_all x1, starting transfers between devices, per_device(): lax.all_to_all(result, 'expert', split_axis=0, concat_axis=0, tiled=True)  4.24 us
    dot_general x1, matrix products, expert_apply(): gate = jnp.dot(rows_in, gate_part, preferred_element_type=jnp.float32)  2.49 us
    dot_general x1, matrix products, per_device(): jnp.dot(place, answered.reshape(-1, width), preferred_element_type=jnp.fl...  2.18 us
    unnamed x8, local copies, waits for them, and re-layouts  1.8 us
  transfers between devices with their start and end apart: 1, of which 1 were waited for; matrix products, arithmetic and copies ran while one was open for 0% of the time, Pallas kernels for 0%

commit v1 on v0

--- a/solution.py
+++ b/solution.py
@@ -1,6 +1,10 @@
+import functools
+
 import jax
 import jax.numpy as jnp
 from jax import lax
+from jax.experimental import pallas as pl
+from jax.experimental.pallas import tpu as pltpu
 from jax.sharding import PartitionSpec as P
 
 
@@ -13,7 +17,7 @@
     )
 
 
-def per_device(tokens, norm_gain, expert_ids, gate_values, w_gate, w_up, w_down):
+def routed_device(tokens, norm_gain, expert_ids, gate_values, w_gate, w_up, w_down):
     rows, width = tokens.shape
     top = expert_ids.shape[1]
     expert_count = lax.axis_size("expert")
@@ -53,6 +57,235 @@
     return jnp.sum(weighted, axis=1).astype(jnp.bfloat16)
 
 
+MESH = pl.DeviceIdType.MESH
+GATE = 128
+CHUNKS = 4
+
+
+def gathered_kernel(
+    tokens_ref, gain_ref, ids_ref, gates_ref, wg_hbm, wu_hbm, wd_hbm, out_ref,
+    buf, wg, wu, wd, acc, hid, part, c_src, c_dst, x_src, x_dst, z_src, z_dst,
+    w_sem, ag_send, ag_recv, rs_send, rs_recv,
+):
+    rows, width = tokens_ref.shape
+    hidden = wg.shape[1]
+    every = buf.shape[0]
+    layers = every // (4 * rows)
+    quarter, half = every // 4, every // 2
+    cut = width // CHUNKS
+
+    group, head = lax.axis_index("groups"), lax.axis_index("head")
+    me = lax.axis_index("expert")
+    z, x, c = me // 4, (me // 2) % 2, me % 2
+
+    def device(dz, dx, dc):
+        zt = (z + dz + layers) % layers
+        xt = (x + dx) % 2
+        ct = (c + dc) % 2
+        return (group, zt * 4 + xt * 2 + ct, head)
+
+    weight_copies = []
+    for k in range(CHUNKS):
+        span = pl.ds(k * cut, cut)
+        for i, (src, dst) in enumerate(((wg_hbm, wg), (wu_hbm, wu))):
+            copy = pltpu.make_async_copy(src.at[0, span], dst.at[span], w_sem.at[i, k])
+            copy.start()
+            weight_copies.append(copy)
+    down_copies = []
+    for k in range(CHUNKS):
+        span = pl.ds(k * cut, cut)
+        copy = pltpu.make_async_copy(wd_hbm.at[0, span], wd.at[span], w_sem.at[2, k])
+        copy.start()
+        down_copies.append(copy)
+
+    partners = [device(dz, 0, 0) for dz in range(1, layers)] + [device(0, 1, 0), device(0, 0, 1)]
+    barrier = pltpu.get_barrier_semaphore()
+    for partner in partners:
+        pl.semaphore_signal(barrier, inc=1, device_id=partner, device_id_type=MESH)
+
+    tokens_f = tokens_ref[...].astype(jnp.float32)
+    scale = lax.rsqrt(jnp.mean(tokens_f * tokens_f, axis=-1, keepdims=True) + 1e-06)
+    buf[0:rows, GATE:] = (tokens_f * scale * gain_ref[...]).astype(jnp.bfloat16)
+    lane = lax.broadcasted_iota(jnp.int32, (rows, GATE), 1)
+    slot = lane % 16
+    ids, gates = ids_ref[...], gates_ref[...]
+    spread = jnp.zeros((rows, GATE), jnp.float32)
+    for k in range(ids.shape[1]):
+        spread += jnp.where(ids[:, k : k + 1] == slot, gates[:, k : k + 1], 0.0)
+    first = spread.astype(jnp.bfloat16).astype(jnp.float32)
+    rest = spread - first
+    second = rest.astype(jnp.bfloat16).astype(jnp.float32)
+    third = rest - second
+    parts = jnp.where(lane < 16, first, jnp.where(lane < 32, second, jnp.where(lane < 48, third, 0.0)))
+    buf[0:rows, 0:GATE] = parts.astype(jnp.bfloat16)
+
+    pl.semaphore_wait(barrier, len(partners))
+
+    def columns(k):
+        return pl.ds(0, GATE + cut) if k == 0 else pl.ds(GATE + k * cut, cut)
+
+    started = []
+
+    def send(src, dst, sems, k, i, target):
+        send_sems, recv_sems = sems
+        copy = pltpu.make_async_remote_copy(
+            src_ref=src, dst_ref=dst, send_sem=send_sems.at[k, i], recv_sem=recv_sems.at[k, i],
+            device_id=target, device_id_type=MESH,
+        )
+        copy.start()
+        started.append(copy)
+        return copy
+
+    gather_sems, scatter_sems = (ag_send, ag_recv), (rs_send, rs_recv)
+
+    def gather(k, i, at, size, to, target):
+        span = columns(k)
+        return send(
+            buf.at[pl.ds(at, size), span], buf.at[pl.ds(to, size), span], gather_sems, k, i, target
+        )
+
+    along_z, along_x, along_c = {}, {}, {}
+    for k in range(CHUNKS):
+        along_z[k] = [
+            gather(k, dz - 1, 0, rows, dz * rows, device(dz, 0, 0)) for dz in range(1, layers)
+        ]
+        along_x[k] = [gather(k, 3, 0, rows, quarter, device(0, 1, 0))]
+
+    def multiply(k):
+        weight_copies[2 * k].wait()
+        weight_copies[2 * k + 1].wait()
+        lhs = buf[:, GATE + k * cut : GATE + (k + 1) * cut]
+        for w, base in ((wg, 0), (wu, hidden)):
+            for n in range(0, hidden, 256):
+                value = jnp.dot(
+                    lhs, w[k * cut : (k + 1) * cut, n : n + 256], preferred_element_type=jnp.float32
+                )
+                at = slice(base + n, base + n + 256)
+                if k == 0:
+                    acc[:, at] = value
+                else:
+                    acc[:, at] += value
+
+    for step in range(CHUNKS + 2):
+        if step < CHUNKS:
+            k = step
+            for copy in along_z[k]:
+                copy.wait_recv()
+            along_x[k].append(
+                gather(k, 4, rows, quarter - rows, quarter + rows, device(0, 1, 0))
+            )
+            along_c[k] = [gather(k, 5, 0, quarter, half, device(0, 0, 1))]
+        if 0 <= step - 1 < CHUNKS:
+            k = step - 1
+            for copy in along_x[k]:
+                copy.wait_recv()
+            along_c[k].append(gather(k, 6, quarter, quarter, half + quarter, device(0, 0, 1)))
+        if 0 <= step - 2 < CHUNKS:
+            k = step - 2
+            for copy in along_c[k]:
+                copy.wait_recv()
+            multiply(k)
+
+    gate, upper = acc[:, 0:hidden], acc[:, hidden:]
+    hid[...] = (gate / (1.0 + jnp.exp(-gate)) * upper).astype(jnp.bfloat16)
+    wide = lax.broadcasted_iota(jnp.int32, (every, GATE), 1)
+    mine = jnp.where(wide % 16 == me, buf[:, 0:GATE].astype(jnp.float32), 0.0)
+    weight = jnp.sum(mine, axis=1, keepdims=True)
+
+    to_core, to_x, to_z = {}, {}, {}
+    for step in range(CHUNKS + 3):
+        if step < CHUNKS:
+            k = step
+            down_copies[k].wait()
+            for n in range(k * cut, (k + 1) * cut, 256):
+                at = slice(n, n + 256)
+                value = lax.dot_general(
+                    hid[...], wd[at, :], (((1,), (1,)), ((), ())),
+                    preferred_element_type=jnp.float32,
+                )
+                value = value * weight
+                c_src[:, at] = value[half:].astype(jnp.bfloat16)
+                part[:, at] = value[:half]
+            span = pl.ds(k * cut, cut)
+            to_core[k] = send(
+                c_src.at[:, span], c_dst.at[:, span], scatter_sems, k, 0, device(0, 0, 1)
+            )
+        if 0 <= step - 1 < CHUNKS:
+            k = step - 1
+            at, span = slice(k * cut, (k + 1) * cut), pl.ds(k * cut, cut)
+            to_core[k].wait_recv()
+            x_src[:, at] = (
+                part[quarter:, at] + c_dst[quarter:, at].astype(jnp.float32)
+            ).astype(jnp.bfloat16)
+            to_x[k] = send(x_src.at[:, span], x_dst.at[:, span], scatter_sems, k, 1, device(0, 1, 0))
+            part[:quarter, at] += c_dst[:quarter, at].astype(jnp.float32)
+        if 0 <= step - 2 < CHUNKS:
+            k = step - 2
+            at, span = slice(k * cut, (k + 1) * cut), pl.ds(k * cut, cut)
+            to_x[k].wait_recv()
+            z_src[:, at] = (
+                part[rows:quarter, at] + x_dst[rows:, at].astype(jnp.float32)
+            ).astype(jnp.bfloat16)
+            to_z[k] = [
+                send(
+                    z_src.at[pl.ds((dz - 1) * rows, rows), span],
+                    z_dst.at[pl.ds((dz - 1) * rows, rows), span],
+                    scatter_sems, k, 1 + dz, device(-dz, 0, 0),
+                )
+                for dz in range(1, layers)
+            ]
+            part[:rows, at] += x_dst[:rows, at].astype(jnp.float32)
+        if 0 <= step - 3 < CHUNKS:
+            k = step - 3
+            at = slice(k * cut, (k + 1) * cut)
+            for copy in to_z[k]:
+                copy.wait_recv()
+            total = part[:rows, at]
+            for dz in range(layers - 1):
+                total += z_dst[dz * rows : (dz + 1) * rows, at].astype(jnp.float32)
+            out_ref[:, at] = total.astype(jnp.bfloat16)
+
+    for copy in started:
+        copy.wait_send()
+
+
+def gathered_device(tokens, norm_gain, expert_ids, gate_values, w_gate, w_up, w_down):
+    rows, width = tokens.shape
+    hidden = w_gate.shape[2]
+    every = rows * lax.axis_size("expert")
+    bf16, f32 = jnp.bfloat16, jnp.float32
+    vmem, hbm = pl.BlockSpec(memory_space=pltpu.VMEM), pl.BlockSpec(memory_space=pl.ANY)
+    return pl.pallas_call(
+        gathered_kernel,
+        out_shape=jax.ShapeDtypeStruct((rows, width), bf16),
+        in_specs=[vmem] * 4 + [hbm] * 3,
+        out_specs=vmem,
+        scratch_shapes=[
+            pltpu.VMEM((every, GATE + width), bf16),
+            pltpu.VMEM((width, hidden), bf16),
+            pltpu.VMEM((width, hidden), bf16),
+            pltpu.VMEM((width, hidden), bf16),
+            pltpu.VMEM((every, 2 * hidden), f32),
+            pltpu.VMEM((every, hidden), bf16),
+            pltpu.VMEM((every // 2, width), f32),
+            pltpu.VMEM((every // 2, width), bf16),
+            pltpu.VMEM((every // 2, width), bf16),
+            pltpu.VMEM((every // 4, width), bf16),
+            pltpu.VMEM((every // 4, width), bf16),
+            pltpu.VMEM((every // 4 - rows, width), bf16),
+            pltpu.VMEM((every // 4 - rows, width), bf16),
+            pltpu.SemaphoreType.DMA((3, CHUNKS)),
+            pltpu.SemaphoreType.DMA((CHUNKS, 7)),
+            pltpu.SemaphoreType.DMA((CHUNKS, 7)),
+            pltpu.SemaphoreType.DMA((CHUNKS, 5)),
+            pltpu.SemaphoreType.DMA((CHUNKS, 5)),
+        ],
+        compiler_params=pltpu.CompilerParams(
+            collective_id=0, has_side_effects=True, vmem_limit_bytes=40 * 1024 * 1024
+        ),
+    )(tokens, norm_gain.reshape(1, width), expert_ids, gate_values, w_gate, w_up, w_down)
+
+
 def solution(mesh):
     in_specs = (
         P(("groups", "expert", "head"), None),
@@ -64,6 +297,9 @@
         P("expert", None, "head"),
     )
     out_specs = P(("groups", "expert", "head"), None)
+    experts = mesh.shape["expert"]
+    dense = mesh.shape["head"] == 1 and experts == 16
+    per_device = gathered_device if dense else routed_device
     return jax.shard_map(
         per_device, mesh=mesh, in_specs=in_specs, out_specs=out_specs, check_vma=False
     )

time: 54.3 us -> 46.8 us (0.86)
  Pallas kernels: 0 us -> 37.1 us
  blocking collectives: 21.6 us -> 0 us
  waiting for transfers between devices: 14.3 us -> 0 us
  matrix products: 9.74 us -> 0 us
  local copies, waits for them, and re-layouts: 1.97 us -> 9.35 us
  starting transfers between devices: 4.24 us -> 0 us
  other arithmetic: 1.94 us -> 0 us
    pallas_call x0 -> x1, Pallas kernels: none -> 37.1 us  [gathered_device(): pl.pallas_call(gathered_kernel, out_shape=jax.ShapeDtypeStruct((rows, wid...]
    all_to_all x1 -> x0, blocking collectives: 21.6 us -> none  [per_device(): lax.all_to_all(outgoing, 'expert', split_axis=0, concat_axis=0, tiled=True)]
    all_to_all x1 -> x0, waiting for transfers between devices: 14.3 us -> none  [per_device(): lax.all_to_all(result, 'expert', split_axis=0, concat_axis=0, tiled=True)]
    dot_general x5 -> x0, matrix products: 9.74 us -> none  [the longest x1 4.51 us: expert_apply(): lax.dot_general(hidden, down_part, (((1,), (1,)), ((), ())), preferred_el...]
    unnamed x8 -> x13, local copies, waits for them, and re-layouts: 1.8 us -> 9.35 us
    all_to_all x1 -> x0, starting transfers between devices: 4.24 us -> none  [per_device(): lax.all_to_all(result, 'expert', split_axis=0, concat_axis=0, tiled=True)]
    reduce_sum x1 -> x0, other arithmetic: 0.98 us -> none  [per_device(): jnp.mean(tokens_f * tokens_f, axis=-1, keepdims=True) + 1e-06]
    convert_element_type x2 -> x0, other arithmetic: 0.94 us -> none  [the longest x1 0.93 us: per_device(): normed = (tokens_f * scale * norm_gain[None, :]).astype(jnp.bfloat16)]
  transfers between devices with their start and end apart: 1 -> 0, of which waited for: 1 -> 0; matrix products, arithmetic and copies ran while one was open for 0% -> 0% of each run, Pallas kernels for 0% -> 0%
where the time goes in v1:
time: 46.8 us; the launch traced here: 46.5 us
  Pallas kernels  37.1 us (79%)
  local copies, waits for them, and re-layouts  9.35 us (20%)
    pallas_call x1, Pallas kernels, gathered_device(): pl.pallas_call(gathered_kernel, out_shape=jax.ShapeDtypeStruct((rows, wid...  37.1 us
    unnamed x13, local copies, waits for them, and re-layouts  9.35 us

profile of v1, /device:TPU:0, one launch (start us, length us, event | category | flops | bytes accessed | tf_op | source)
XLA Modules:
  0.0 46.5 jit_solution(13956871234231808926)
XLA Ops:
  0.0 0.8 %copy.8.ids_ref = s32[16,8]{1,0:T(8,128)S(1)} copy(s32[16,8]{0,1:T(8,128)} %param.9) | data formatting | bytes 1024 | tf_op args[2]
  0.8 0.8 %copy.9.gates_ref = f32[16,8]{1,0:T(8,128)S(1)} copy(f32[16,8]{0,1:T(8,128)} %param.10) | data formatting | bytes 1024 | tf_op args[3]
  1.5 0.0 copy-start
  1.5 1.9 %copy-done = bf16[1,2048,768]{2,1,0:T(8,128)(2,1)S(1)} copy-done((bf16[1,2048,768]{2,1,0:T(8,128)(2,1)S(1)}, bf16[1,2048,768]{2,1,0:T(8,128)(2,1)}, u32[]{:S(2)}) %copy-start) | copy-done | bytes 3145752
  3.4 0.0 copy-start.1
  3.4 1.9 %copy-done.1 = bf16[1,2048,768]{2,1,0:T(8,128)(2,1)S(1)} copy-done((bf16[1,2048,768]{2,1,0:T(8,128)(2,1)S(1)}, bf16[1,2048,768]{2,1,0:T(8,128)(2,1)}, u32[]{:S(2)}) %copy-start.1) | copy-done | bytes 3145752
  5.3 0.0 copy-start.2
  5.3 1.9 %copy-done.2 = bf16[1,2048,768]{2,1,0:T(8,128)(2,1)S(1)} copy-done((bf16[1,2048,768]{2,1,0:T(8,128)(2,1)S(1)}, bf16[1,2048,768]{2,1,0:T(8,128)(2,1)}, u32[]{:S(2)}) %copy-start.2) | copy-done | bytes 3145752
  7.2 0.0 copy-start.3
  7.2 0.8 %copy-done.3 = bf16[16,2048]{1,0:T(8,128)(2,1)S(1)} copy-done((bf16[16,2048]{1,0:T(8,128)(2,1)S(1)}, bf16[16,2048]{1,0:T(8,128)(2,1)}, u32[]{:S(2)}) %copy-start.3) | copy-done | bytes 65560
  8.0 0.0 copy-start.4
  8.0 0.7 %copy-done.4 = f32[2048]{0:T(1024)S(1)} copy-done((f32[2048]{0:T(1024)S(1)}, f32[2048]{0:T(1024)}, u32[]{:S(2)}) %copy-start.4) | copy-done | bytes 8216
  8.7 37.1 %shard_map.73 = bf16[16,2048]{1,0:T(8,128)(2,1)S(1)} custom-call(bf16[16,2048]{1,0:T(8,128)(2,1)S(1)} %copy-done.3, f32[1,2048]{1,0:T(1,128)S(1)} %bitcast.1, s32[16,8]{1,0:T(8,128)S(1)} %copy.8.ids_ref, f32[16,8]{1,0:T(8,128)S(1)} %copy.9.gates_ref, bf16[1,2048,768]{2,1,0:T(8,128)(2,1)S(1)} %copy-done, bf16[1,2048,768]{2,1,0:T(8,128)(2,1)S(1)} %copy-done.1, ...), custom_call_target="tpu_custom_call" | custom-call | tf_op jit(solution)/shard_map/pallas_call | solution.py:258
  45.8 0.6 %copy.11 = bf16[16,2048]{1,0:T(8,128)(2,1)} copy(bf16[16,2048]{1,0:T(8,128)(2,1)S(1)} %shard_map.73) | data formatting | bytes 131072
Async XLA Ops:
  1.5 1.9 %copy-start = (bf16[1,2048,768]{2,1,0:T(8,128)(2,1)S(1)}, bf16[1,2048,768]{2,1,0:T(8,128)(2,1)}, u32[]{:S(2)}) copy-start(bf16[1,2048,768]{2,1,0:T(8,128)(2,1)} %wg_hbm.1) | copy-start | bytes 9437188
  3.4 1.9 %copy-start.1 = (bf16[1,2048,768]{2,1,0:T(8,128)(2,1)S(1)}, bf16[1,2048,768]{2,1,0:T(8,128)(2,1)}, u32[]{:S(2)}) copy-start(bf16[1,2048,768]{2,1,0:T(8,128)(2,1)} %wu_hbm.1) | copy-start | bytes 9437188
  5.3 1.9 %copy-start.2 = (bf16[1,2048,768]{2,1,0:T(8,128)(2,1)S(1)}, bf16[1,2048,768]{2,1,0:T(8,128)(2,1)}, u32[]{:S(2)}) copy-start(bf16[1,2048,768]{2,1,0:T(8,128)(2,1)} %wd_hbm.1) | copy-start | bytes 9437188
  7.2 0.8 %copy-start.3 = (bf16[16,2048]{1,0:T(8,128)(2,1)S(1)}, bf16[16,2048]{1,0:T(8,128)(2,1)}, u32[]{:S(2)}) copy-start(bf16[16,2048]{1,0:T(8,128)(2,1)} %tokens_ref.1) | copy-start | bytes 196612
  8.0 0.7 %copy-start.4 = (f32[2048]{0:T(1024)S(1)}, f32[2048]{0:T(1024)}, u32[]{:S(2)}) copy-start(f32[2048]{0:T(1024)} %param.8) | copy-start | bytes 24580

commit v2 on v0

--- a/solution.py
+++ b/solution.py
@@ -1,6 +1,10 @@
+import functools
+
 import jax
 import jax.numpy as jnp
 from jax import lax
+from jax.experimental import pallas as pl
+from jax.experimental.pallas import tpu as pltpu
 from jax.sharding import PartitionSpec as P
 
 
@@ -13,7 +17,7 @@
     )
 
 
-def per_device(tokens, norm_gain, expert_ids, gate_values, w_gate, w_up, w_down):
+def routed_device(tokens, norm_gain, expert_ids, gate_values, w_gate, w_up, w_down):
     rows, width = tokens.shape
     top = expert_ids.shape[1]
     expert_count = lax.axis_size("expert")
@@ -53,6 +57,266 @@
     return jnp.sum(weighted, axis=1).astype(jnp.bfloat16)
 
 
+MESH = pl.DeviceIdType.MESH
+GATE = 128
+TILE = 256
+
+
+def gathered_kernel(
+    tokens_hbm, gain_hbm, ids_hbm, gates_hbm, wg_hbm, wu_hbm, wd_hbm, out_ref,
+    tokens_ref, gain_ref, ids_ref, gates_ref,
+    buf, wg, wu, wd, hid, part, c_src, c_dst, x_src, x_dst, z_src, z_dst,
+    zb_src, zb_dst, xb_src, xb_dst,
+    in_sem, w_sem, send_sem, recv_sem,
+):
+    rows, width = tokens_ref.shape
+    hidden = wg.shape[1]
+    half = 8 * rows
+    bf16, f32 = jnp.bfloat16, jnp.float32
+
+    group, head = lax.axis_index("groups"), lax.axis_index("head")
+    me = lax.axis_index("expert")
+    z, x, c = me // 4, (me // 2) % 2, me % 2
+    layer = [z, z + 1 - 2 * (z % 2), (z + 2) % 4, 3 - z]
+
+    def device(far=0, dx=0, dc=0):
+        return (group, layer[far] * 4 + ((x + dx) % 2) * 2 + (c + dc) % 2, head)
+
+    partners = [device(3), device(2), device(1), device(0, 1), device(0, 0, 1)]
+    barrier = pltpu.get_barrier_semaphore()
+    for partner in partners:
+        pl.semaphore_signal(barrier, inc=1, device_id=partner, device_id_type=MESH)
+
+    pairs = (
+        (tokens_hbm, tokens_ref), (gain_hbm, gain_ref), (ids_hbm, ids_ref), (gates_hbm, gates_ref)
+    )
+    inputs = [pltpu.make_async_copy(s, d, in_sem.at[i]) for i, (s, d) in enumerate(pairs)]
+    for copy in inputs:
+        copy.start()
+    weights = []
+    for i, (src, dst) in enumerate(((wg_hbm, wg), (wu_hbm, wu), (wd_hbm, wd))):
+        for k in range(4):
+            span = pl.ds(k * (width // 4), width // 4)
+            weights.append(pltpu.make_async_copy(src.at[0, span], dst.at[span], w_sem.at[i, k]))
+    for copy in weights:
+        copy.start()
+
+    for copy in inputs:
+        copy.wait()
+    tokens_f = tokens_ref[...].astype(f32)
+    scale = lax.rsqrt(jnp.mean(tokens_f * tokens_f, axis=-1, keepdims=True) + 1e-06)
+    buf[0:rows, GATE:] = (tokens_f * scale * gain_ref[...]).astype(bf16)
+    line = lax.broadcasted_iota(jnp.int32, (GATE, rows), 0)
+    ids, gates = ids_ref[...], gates_ref[...]
+    spread = jnp.zeros((GATE, rows), f32)
+    for k in range(ids.shape[0]):
+        spread += jnp.where(ids[k : k + 1, :] == line % 16, gates[k : k + 1, :], 0.0)
+    first = spread.astype(bf16).astype(f32)
+    rest = spread - first
+    middle = rest.astype(bf16).astype(f32)
+    third = rest - middle
+    split = jnp.where(
+        line < 16, first, jnp.where(line < 32, middle, jnp.where(line < 48, third, 0.0))
+    )
+    unit = lax.broadcasted_iota(jnp.int32, (rows, rows), 0) == lax.broadcasted_iota(
+        jnp.int32, (rows, rows), 1
+    )
+    buf[0:rows, 0:GATE] = lax.dot_general(
+        unit.astype(f32).astype(bf16), split.astype(bf16), (((1,), (1,)), ((), ())),
+        preferred_element_type=f32,
+    ).astype(bf16)
+
+    pl.semaphore_wait(barrier, len(partners))
+
+    started = []
+
+    def send(src, dst, target):
+        i = len(started)
+        copy = pltpu.make_async_remote_copy(
+            src_ref=src, dst_ref=dst, send_sem=send_sem.at[i], recv_sem=recv_sem.at[i],
+            device_id=target, device_id_type=MESH,
+        )
+        copy.start()
+        started.append(copy)
+        return copy
+
+    def gather(at, size, to, target, span=None):
+        span = pl.ds(0, GATE + width) if span is None else span
+        return send(buf.at[pl.ds(at, size), span], buf.at[pl.ds(to, size), span], target)
+
+    def arrive(copies):
+        for copy in copies:
+            copy.wait_recv()
+
+    two, four, mid = 2 * rows, 4 * rows, width // 2
+    first_half, second_half = pl.ds(0, GATE + mid), pl.ds(GATE + mid, mid)
+    place = {1: rows, 3: half, 2: half + rows}
+    x_second = gather(0, rows, two, device(0, 1), second_half)
+    z_first = {f: gather(0, rows, place[f], device(f), first_half) for f in (1, 3, 2)}
+    x_first = [gather(0, rows, two, device(0, 1), first_half)]
+    z_second = {f: [gather(0, rows, place[f], device(f), second_half)] for f in (2, 3, 1)}
+    x_second.wait_recv()
+    for f in (2, 3, 1):
+        z_second[f].append(gather(two, rows, place[f] + two, device(f), second_half))
+    far_x = []
+    z_first[1].wait_recv()
+    x_first.append(gather(rows, rows, two + rows, device(0, 1), first_half))
+    for f in (3, 2):
+        z_first[f].wait_recv()
+        far_x.append(gather(place[f], rows, place[f] + two, device(0, 1), first_half))
+    arrive(x_first)
+    arrive(z_second[1])
+    near_c = gather(0, four, four, device(0, 0, 1))
+    for copy in weights:
+        copy.wait()
+    near_c.wait_recv()
+
+    def project(h):
+        at = slice(h * half, (h + 1) * half)
+        for n in range(0, hidden, TILE):
+            lhs = buf[at, GATE:]
+            gate = jnp.dot(lhs, wg[:, n : n + TILE], preferred_element_type=f32)
+            upper = jnp.dot(lhs, wu[:, n : n + TILE], preferred_element_type=f32)
+            hid[at, n : n + TILE] = (gate / (1.0 + jnp.exp(-gate)) * upper).astype(bf16)
+        wide = lax.broadcasted_iota(jnp.int32, (half, GATE), 1)
+        mine = jnp.where(wide % 16 == me, buf[at, 0:GATE].astype(f32), 0.0)
+        return jnp.sum(mine, axis=1, keepdims=True)
+
+    def answer(h, weight, lo):
+        mine = slice(h * four, (h + 1) * four)
+        for n in range(lo, lo + mid, TILE):
+            value = lax.dot_general(
+                hid[h * half : (h + 1) * half, :], wd[n : n + TILE, :], (((1,), (1,)), ((), ())),
+                preferred_element_type=f32,
+            )
+            value = value * weight
+            c_src[mine, n : n + TILE] = value[four:].astype(bf16)
+            part[mine, n : n + TILE] = value[:four]
+        block = (pl.ds(h * four, four), pl.ds(lo, mid))
+        return send(c_src.at[block], c_dst.at[block], device(0, 0, 1))
+
+    def cross(h):
+        base = h * four
+        x_src[h * two : (h + 1) * two, :] = (
+            part[base + two : base + four, :mid] + c_dst[base + two : base + four, :mid].astype(f32)
+        ).astype(bf16)
+        block = pl.ds(h * two, two)
+        copy = send(x_src.at[block], x_dst.at[block], device(0, 1))
+        part[base : base + two, :mid] += c_dst[base : base + two, :mid].astype(f32)
+        return copy
+
+    def along_first(far):
+        at = {1: rows, 3: four, 2: four + rows}[far]
+        got = {1: rows, 3: two, 2: two + rows}[far]
+        out = slice((far - 1) * rows, far * rows)
+        z_src[out, :] = (
+            part[at : at + rows, :mid] + x_dst[got : got + rows, :].astype(f32)
+        ).astype(bf16)
+        block = pl.ds((far - 1) * rows, rows)
+        return send(z_src.at[block], z_dst.at[block], device(far))
+
+    def along_second(far):
+        at = {1: rows, 3: four, 2: four + rows}[far]
+        base = (far - 1) * two
+        for i in range(2):
+            row = slice(at + i * two, at + i * two + rows)
+            zb_src[base + i * rows : base + (i + 1) * rows, :] = (
+                part[row, mid:] + c_dst[row, mid:].astype(f32)
+            ).astype(bf16)
+        block = pl.ds(base, two)
+        return send(zb_src.at[block], zb_dst.at[block], device(far))
+
+    near_weight = project(0)
+    arrive(far_x)
+    arrive(z_second[3] + z_second[2])
+    far_c = gather(half, four, half + four, device(0, 0, 1))
+    near_back = [answer(0, near_weight, lo) for lo in (mid, 0)]
+    far_c.wait_recv()
+    far_weight = project(1)
+    far_back = [answer(1, far_weight, mid)]
+    near_back[0].wait_recv()
+    second = {1: along_second(1)}
+    near_back[1].wait_recv()
+    near_cross = cross(0)
+    far_back.append(answer(1, far_weight, 0))
+    far_back[0].wait_recv()
+    for far in (2, 3):
+        second[far] = along_second(far)
+    far_back[1].wait_recv()
+    far_cross = cross(1)
+    near_cross.wait_recv()
+    last = [along_first(1)]
+    part[0:rows, :mid] += x_dst[0:rows, :].astype(f32)
+    own = [
+        part[i * two : i * two + rows, mid:] + c_dst[i * two : i * two + rows, mid:].astype(f32)
+        for i in range(2)
+    ]
+    for far in (1, 3, 2):
+        second[far].wait_recv()
+        for i in range(2):
+            at = (far - 1) * two + i * rows
+            own[i] += zb_dst[at : at + rows, :].astype(f32)
+    xb_src[...] = own[1].astype(bf16)
+    second_cross = send(xb_src, xb_dst, device(0, 1))
+    far_cross.wait_recv()
+    last.extend([along_first(2), along_first(3)])
+    second_cross.wait_recv()
+    out_ref[:, mid:] = (own[0] + xb_dst[...].astype(f32)).astype(bf16)
+    arrive(last)
+    total = part[0:rows, :mid]
+    for i in range(3):
+        total += z_dst[i * rows : (i + 1) * rows, :].astype(f32)
+    out_ref[:, :mid] = total.astype(bf16)
+
+    for copy in started:
+        copy.wait_send()
+
+
+def gathered_device(tokens, norm_gain, expert_ids, gate_values, w_gate, w_up, w_down):
+    rows, width = tokens.shape
+    top = expert_ids.shape[1]
+    hidden = w_gate.shape[2]
+    every = rows * 16
+    bf16, f32 = jnp.bfloat16, jnp.float32
+    vmem, hbm = pl.BlockSpec(memory_space=pltpu.VMEM), pl.BlockSpec(memory_space=pl.ANY)
+    copies, mid = 29, width // 2
+    return pl.pallas_call(
+        gathered_kernel,
+        out_shape=jax.ShapeDtypeStruct((rows, width), bf16),
+        in_specs=[hbm] * 7,
+        out_specs=vmem,
+        scratch_shapes=[
+            pltpu.VMEM((rows, width), bf16),
+            pltpu.VMEM((1, width), f32),
+            pltpu.VMEM((top, rows), jnp.int32),
+            pltpu.VMEM((top, rows), f32),
+            pltpu.VMEM((every, GATE + width), bf16),
+            pltpu.VMEM((width, hidden), bf16),
+            pltpu.VMEM((width, hidden), bf16),
+            pltpu.VMEM((width, hidden), bf16),
+            pltpu.VMEM((every, hidden), bf16),
+            pltpu.VMEM((every // 2, width), f32),
+            pltpu.VMEM((every // 2, width), bf16),
+            pltpu.VMEM((every // 2, width), bf16),
+            pltpu.VMEM((every // 4, mid), bf16),
+            pltpu.VMEM((every // 4, mid), bf16),
+            pltpu.VMEM((3 * rows, mid), bf16),
+            pltpu.VMEM((3 * rows, mid), bf16),
+            pltpu.VMEM((6 * rows, mid), bf16),
+            pltpu.VMEM((6 * rows, mid), bf16),
+            pltpu.VMEM((rows, mid), bf16),
+            pltpu.VMEM((rows, mid), bf16),
+            pltpu.SemaphoreType.DMA((4,)),
+            pltpu.SemaphoreType.DMA((3, 4)),
+            pltpu.SemaphoreType.DMA((copies,)),
+            pltpu.SemaphoreType.DMA((copies,)),
+        ],
+        compiler_params=pltpu.CompilerParams(
+            collective_id=0, has_side_effects=True, vmem_limit_bytes=61 * 1024 * 1024
+        ),
+    )(tokens, norm_gain.reshape(1, width), expert_ids.T, gate_values.T, w_gate, w_up, w_down)
+
+
 def solution(mesh):
     in_specs = (
         P(("groups", "expert", "head"), None),
@@ -64,6 +328,9 @@
         P("expert", None, "head"),
     )
     out_specs = P(("groups", "expert", "head"), None)
+    experts = mesh.shape["expert"]
+    dense = mesh.shape["head"] == 1 and experts == 16
+    per_device = gathered_device if dense else routed_device
     return jax.shard_map(
         per_device, mesh=mesh, in_specs=in_specs, out_specs=out_specs, check_vma=False
     )

time: 54.3 us -> 35.5 us (0.65)
  Pallas kernels: 0 us -> 33.9 us
  blocking collectives: 21.6 us -> 0 us
  waiting for transfers between devices: 14.3 us -> 0 us
  matrix products: 9.74 us -> 0 us
  starting transfers between devices: 4.24 us -> 0 us
  other arithmetic: 1.94 us -> 0 us
    pallas_call x0 -> x1, Pallas kernels: none -> 33.9 us  [gathered_device(): pl.pallas_call(gathered_kernel, out_shape=jax.ShapeDtypeStruct((rows, wid...]
    all_to_all x1 -> x0, blocking collectives: 21.6 us -> none  [per_device(): lax.all_to_all(outgoing, 'expert', split_axis=0, concat_axis=0, tiled=True)]
    all_to_all x1 -> x0, waiting for transfers between devices: 14.3 us -> none  [per_device(): lax.all_to_all(result, 'expert', split_axis=0, concat_axis=0, tiled=True)]
    dot_general x5 -> x0, matrix products: 9.74 us -> none  [the longest x1 4.51 us: expert_apply(): lax.dot_general(hidden, down_part, (((1,), (1,)), ((), ())), preferred_el...]
    all_to_all x1 -> x0, starting transfers between devices: 4.24 us -> none  [per_device(): lax.all_to_all(result, 'expert', split_axis=0, concat_axis=0, tiled=True)]
    reduce_sum x1 -> x0, other arithmetic: 0.98 us -> none  [per_device(): jnp.mean(tokens_f * tokens_f, axis=-1, keepdims=True) + 1e-06]
    convert_element_type x2 -> x0, other arithmetic: 0.94 us -> none  [the longest x1 0.93 us: per_device(): normed = (tokens_f * scale * norm_gain[None, :]).astype(jnp.bfloat16)]
    unnamed x8 -> x1, local copies, waits for them, and re-layouts: 1.8 us -> 1.47 us
  transfers between devices with their start and end apart: 1 -> 0, of which waited for: 1 -> 0; matrix products, arithmetic and copies ran while one was open for 0% -> 0% of each run, Pallas kernels for 0% -> 0%
where the time goes in v2:
time: 35.5 us; the launch traced here: 35.4 us
  Pallas kernels  33.9 us (95%)
  local copies, waits for them, and re-layouts  1.47 us (4%)
    pallas_call x1, Pallas kernels, gathered_device(): pl.pallas_call(gathered_kernel, out_shape=jax.ShapeDtypeStruct((rows, wid...  33.9 us
    unnamed x1, local copies, waits for them, and re-layouts  1.47 us

profile of v2, /device:TPU:0, one launch (start us, length us, event | category | flops | bytes accessed | tf_op | source)
XLA Modules:
  0.0 35.4 jit_solution(7490382231984069315)
XLA Ops:
  0.0 33.9 %shard_map.73 = bf16[16,2048]{1,0:T(8,128)(2,1)} custom-call(bf16[16,2048]{1,0:T(8,128)(2,1)} %tokens_hbm.1, f32[1,2048]{1,0:T(1,128)} %bitcast.3, s32[8,16]{1,0:T(8,128)} %bitcast.4, f32[8,16]{1,0:T(8,128)} %bitcast.5, bf16[1,2048,768]{2,1,0:T(8,128)(2,1)} %wg_hbm.1, bf16[1,2048,768]{2,1,0:T(8,128)(2,1)} %wu_hbm.1, bf16[1,2048,768]{2,1,0:T(8,128)(2,1)} %wd_hbm.1), custom_call_target="tpu_custom_call" | custom-call | tf_op jit(solution)/shard_map/pallas_call | solution.py:283
  33.9 1.5 %copy.9 = bf16[16,2048]{1,0:T(8,128)(2,1)} copy(bf16[16,2048]{1,0:T(8,128)(2,1)} %shard_map.73) | data formatting | bytes 131072

commit v3 on v2

--- a/solution.py
+++ b/solution.py
@@ -59,6 +59,7 @@
 
 MESH = pl.DeviceIdType.MESH
 GATE = 128
+FIRST = 6
 TILE = 256
 
 
@@ -98,8 +99,6 @@
         for k in range(4):
             span = pl.ds(k * (width // 4), width // 4)
             weights.append(pltpu.make_async_copy(src.at[0, span], dst.at[span], w_sem.at[i, k]))
-    for copy in weights:
-        copy.start()
 
     for copy in inputs:
         copy.wait()
@@ -148,13 +147,16 @@
         for copy in copies:
             copy.wait_recv()
 
-    two, four, mid = 2 * rows, 4 * rows, width // 2
-    first_half, second_half = pl.ds(0, GATE + mid), pl.ds(GATE + mid, mid)
+    two, four, mid = 2 * rows, 4 * rows, width * FIRST // 8
+    tail = width - mid
+    first_half, second_half = pl.ds(0, GATE + mid), pl.ds(GATE + mid, tail)
     place = {1: rows, 3: half, 2: half + rows}
     x_second = gather(0, rows, two, device(0, 1), second_half)
     z_first = {f: gather(0, rows, place[f], device(f), first_half) for f in (1, 3, 2)}
     x_first = [gather(0, rows, two, device(0, 1), first_half)]
     z_second = {f: [gather(0, rows, place[f], device(f), second_half)] for f in (2, 3, 1)}
+    for copy in weights:
+        copy.start()
     x_second.wait_recv()
     for f in (2, 3, 1):
         z_second[f].append(gather(two, rows, place[f] + two, device(f), second_half))
@@ -184,7 +186,8 @@
 
     def answer(h, weight, lo):
         mine = slice(h * four, (h + 1) * four)
-        for n in range(lo, lo + mid, TILE):
+        size = tail if lo else mid
+        for n in range(lo, lo + size, TILE):
             value = lax.dot_general(
                 hid[h * half : (h + 1) * half, :], wd[n : n + TILE, :], (((1,), (1,)), ((), ())),
                 preferred_element_type=f32,
@@ -192,7 +195,7 @@
             value = value * weight
             c_src[mine, n : n + TILE] = value[four:].astype(bf16)
             part[mine, n : n + TILE] = value[:four]
-        block = (pl.ds(h * four, four), pl.ds(lo, mid))
+        block = (pl.ds(h * four, four), pl.ds(lo, size))
         return send(c_src.at[block], c_dst.at[block], device(0, 0, 1))
 
     def cross(h):
@@ -279,7 +282,8 @@
     every = rows * 16
     bf16, f32 = jnp.bfloat16, jnp.float32
     vmem, hbm = pl.BlockSpec(memory_space=pltpu.VMEM), pl.BlockSpec(memory_space=pl.ANY)
-    copies, mid = 29, width // 2
+    copies, mid = 29, width * FIRST // 8
+    tail = width - mid
     return pl.pallas_call(
         gathered_kernel,
         out_shape=jax.ShapeDtypeStruct((rows, width), bf16),
@@ -302,10 +306,10 @@
             pltpu.VMEM((every // 4, mid), bf16),
             pltpu.VMEM((3 * rows, mid), bf16),
             pltpu.VMEM((3 * rows, mid), bf16),
-            pltpu.VMEM((6 * rows, mid), bf16),
-            pltpu.VMEM((6 * rows, mid), bf16),
-            pltpu.VMEM((rows, mid), bf16),
-            pltpu.VMEM((rows, mid), bf16),
+            pltpu.VMEM((6 * rows, tail), bf16),
+            pltpu.VMEM((6 * rows, tail), bf16),
+            pltpu.VMEM((rows, tail), bf16),
+            pltpu.VMEM((rows, tail), bf16),
             pltpu.SemaphoreType.DMA((4,)),
             pltpu.SemaphoreType.DMA((3, 4)),
             pltpu.SemaphoreType.DMA((copies,)),

time: 35.5 us -> 33 us (0.930)
  Pallas kernels: 33.9 us -> 31.3 us
    pallas_call x1, Pallas kernels: 33.9 us -> 31.3 us  [gathered_device(): pl.pallas_call(gathered_kernel, out_shape=jax.ShapeDtypeStruct((rows, wid...]
where the time goes in v3:
time: 33 us; the launch traced here: 32.8 us
  Pallas kernels  31.3 us (95%)
  local copies, waits for them, and re-layouts  1.47 us (4%)
    pallas_call x1, Pallas kernels, gathered_device(): pl.pallas_call(gathered_kernel, out_shape=jax.ShapeDtypeStruct((rows, wid...  31.3 us
    unnamed x1, local copies, waits for them, and re-layouts  1.47 us

profile of v3, /device:TPU:0, one launch (start us, length us, event | category | flops | bytes accessed | tf_op | source)
XLA Modules:
  0.0 32.8 jit_solution(12277868220019237819)
XLA Ops:
  0.0 31.3 %shard_map.73 = bf16[16,2048]{1,0:T(8,128)(2,1)} custom-call(bf16[16,2048]{1,0:T(8,128)(2,1)} %tokens_hbm.1, f32[1,2048]{1,0:T(1,128)} %bitcast.3, s32[8,16]{1,0:T(8,128)} %bitcast.4, f32[8,16]{1,0:T(8,128)} %bitcast.5, bf16[1,2048,768]{2,1,0:T(8,128)(2,1)} %wg_hbm.1, bf16[1,2048,768]{2,1,0:T(8,128)(2,1)} %wu_hbm.1, bf16[1,2048,768]{2,1,0:T(8,128)(2,1)} %wd_hbm.1), custom_call_target="tpu_custom_call" | custom-call | tf_op jit(solution)/shard_map/pallas_call | solution.py:287
  31.3 1.5 %copy.9 = bf16[16,2048]{1,0:T(8,128)(2,1)} copy(bf16[16,2048]{1,0:T(8,128)(2,1)} %shard_map.73) | data formatting | bytes 131072

commit v4 on v3

--- a/solution.py
+++ b/solution.py
@@ -152,7 +152,7 @@
     first_half, second_half = pl.ds(0, GATE + mid), pl.ds(GATE + mid, tail)
     place = {1: rows, 3: half, 2: half + rows}
     x_second = gather(0, rows, two, device(0, 1), second_half)
-    z_first = {f: gather(0, rows, place[f], device(f), first_half) for f in (1, 3, 2)}
+    z_first = {f: gather(0, rows, place[f], device(f), first_half) for f in (2, 3, 1)}
     x_first = [gather(0, rows, two, device(0, 1), first_half)]
     z_second = {f: [gather(0, rows, place[f], device(f), second_half)] for f in (2, 3, 1)}
     for copy in weights:

time: 33 us -> 32.8 us (level)
  no operation moved by 1% of the time
where the time goes in v4:
time: 32.8 us; the launch traced here: 32.6 us
  Pallas kernels  31.1 us (95%)
  local copies, waits for them, and re-layouts  1.47 us (4%)
    pallas_call x1, Pallas kernels, gathered_device(): pl.pallas_call(gathered_kernel, out_shape=jax.ShapeDtypeStruct((rows, wid...  31.1 us
    unnamed x1, local copies, waits for them, and re-layouts  1.47 us

profile of v4, /device:TPU:0, one launch (start us, length us, event | category | flops | bytes accessed | tf_op | source)
XLA Modules:
  0.0 32.6 jit_solution(4433308087473981604)
XLA Ops:
  0.0 31.1 %shard_map.73 = bf16[16,2048]{1,0:T(8,128)(2,1)} custom-call(bf16[16,2048]{1,0:T(8,128)(2,1)} %tokens_hbm.1, f32[1,2048]{1,0:T(1,128)} %bitcast.3, s32[8,16]{1,0:T(8,128)} %bitcast.4, f32[8,16]{1,0:T(8,128)} %bitcast.5, bf16[1,2048,768]{2,1,0:T(8,128)(2,1)} %wg_hbm.1, bf16[1,2048,768]{2,1,0:T(8,128)(2,1)} %wu_hbm.1, bf16[1,2048,768]{2,1,0:T(8,128)(2,1)} %wd_hbm.1), custom_call_target="tpu_custom_call" | custom-call | tf_op jit(solution)/shard_map/pallas_call | solution.py:287
  31.1 1.5 %copy.9 = bf16[16,2048]{1,0:T(8,128)(2,1)} copy(bf16[16,2048]{1,0:T(8,128)(2,1)} %shard_map.73) | data formatting | bytes 131072
